TPU v7x, 32 devices: a whole 2x2x4 slice. The times are simulated.
32 devices in a mesh: pipe: 4 (over y, core), ctx: 8 (over z, x).
Axes of the slice: x: 2, y: 2, z: 4, core: 2. Of those that a mesh axis runs over, the one named last changes fastest.
Arguments:
- incoming: bfloat16 [4, 1024, 1024], P('pipe', 'ctx'), may hold values from -6 to 6
- fresh: bfloat16 [1024, 1024], P('ctx'), may hold values from -6 to 6
- w_uvqk: bfloat16 [4, 1024, 2048], P('pipe'), may hold values from -0.1875 to 0.1875
- w_out: bfloat16 [4, 512, 1024], P('pipe'), may hold values from -0.25 to 0.25
- cache_kv: bfloat16 [4, 2, 128, 1024], P('pipe', None, 'ctx'), may hold values from -6 to 6
- rows_user: int32 [5, 1024], P(None, 'ctx'), may hold values from 0 to 3, never falling along the last dimension, each value on 1 to 512 neighbouring positions
- cache_len: int32 [5, 4], replicated, may hold values from 1 to 64, 128 in all within a row
Outputs:
- section_out: bfloat16 [4, 2, 1024, 1024], P('pipe', None, 'ctx')
Inputs may be any that keep to these rules, and one draw needn't show every extreme that they name: `rows_user`: each micro-batch's row users never fall along the events; every user has at least one event. `cache_len`: each micro-batch's row sums to 128.
All inputs are finite; a program needn't handle non-finite values.
Results may differ from a plain program's by a relative error of at most 0.0085.
Values may be sent and summed in bfloat16 or wider, within the bound.
A program may use at most 64 MiB of HBM per device.

v0:
```python
import math

import jax
import jax.numpy as jnp
from jax import lax
from jax.sharding import PartitionSpec as P

HEADS = 4
STEPS = 2


def passed_along(block, axis, distance):
    devices = range(lax.axis_size(axis))
    route = [(i - distance, i) for i in devices if i - distance in devices]
    return lax.ppermute(block, axis, route)


def normalize(values):
    center = jnp.mean(values, axis=-1, keepdims=True)
    shifted = values - center
    spread = jnp.mean(shifted * shifted, axis=-1, keepdims=True)
    return shifted * lax.rsqrt(spread + 1e-06)


def owners(positions, lengths):
    bounds = jnp.cumsum(lengths)
    return jnp.sum((positions[:, None] >= bounds[None, :-1]).astype(jnp.int32), axis=1)


def attend(queries, kv_rows, allowed):
    width = kv_rows.shape[1] // 2
    count = kv_rows.shape[0]
    key_part = kv_rows[:, :width].reshape(count, HEADS, -1)
    value_part = kv_rows[:, width:].reshape(count, HEADS, -1)
    scale = queries.shape[2] ** (-0.5)
    scores = jnp.einsum("thd,nhd->htn", queries, key_part, preferred_element_type=jnp.float32)
    weights = (jax.nn.silu(scale * scores) * allowed[None].astype(jnp.float32)).astype(jnp.bfloat16)
    summed = jnp.einsum("htn,nhd->thd", weights, value_part, preferred_element_type=jnp.float32)
    return summed.reshape(queries.shape[0], width)


def cache_blocks(attn, all_rows, queries, users, lengths):
    block_rows = math.gcd(all_rows.shape[0], 128)
    blocks = all_rows.reshape(-1, block_rows, all_rows.shape[1])

    def scan_body(total, packed):
        order, segment = packed
        positions = order * block_rows + jnp.arange(block_rows, dtype=jnp.int32)
        allowed = users[:, None] == owners(positions, lengths)[None, :]
        addition = attend(queries, segment, allowed)
        return (total + addition, None)

    result, unused = lax.scan(
        scan_body, attn, (jnp.arange(blocks.shape[0], dtype=jnp.int32), blocks)
    )
    return result


def body(incoming, fresh, w_uvqk, w_out, cache_kv, rows_user, cache_len):
    section = lax.axis_index("pipe")
    sections = lax.axis_size("pipe")
    local_rows = fresh.shape[0]
    width = w_out.shape[1]
    weights_in = w_uvqk[0]
    weights_back = w_out[0]
    fetched = lax.all_gather(cache_kv[0], "ctx", axis=1, tiled=True)
    row_index = jnp.arange(local_rows, dtype=jnp.int32)
    causal = row_index[None, :] <= row_index[:, None]
    results = []
    current = incoming[0]
    for step_index in range(STEPS):
        if step_index > 0:
            passed = passed_along(results[-1], "pipe", 1)
            current = jnp.where(section == 0, fresh, passed)
        batch_index = sections - 1 - section + step_index
        users = lax.dynamic_index_in_dim(rows_user, batch_index, 0, keepdims=False)
        lengths = lax.dynamic_index_in_dim(cache_len, batch_index, 0, keepdims=False)
        normed = normalize(current.astype(jnp.float32)).astype(jnp.bfloat16)
        projected = jax.nn.silu(
            jnp.dot(normed, weights_in, preferred_element_type=jnp.float32)
        ).astype(jnp.bfloat16)
        gate_u = projected[:, :width]
        queries = projected[:, width : 2 * width].reshape(local_rows, HEADS, -1)
        same_user = users[:, None] == users[None, :]
        attn = attend(queries, projected[:, 2 * width :], causal & same_user)
        all_rows = fetched[step_index]
        attn = cache_blocks(attn, all_rows, queries, users, lengths)
        mixed = (normalize(attn) * gate_u.astype(jnp.float32)).astype(jnp.bfloat16)
        result = (
            jnp.dot(mixed, weights_back, preferred_element_type=jnp.float32)
            + current.astype(jnp.float32)
        ).astype(jnp.bfloat16)
        results.append(result)
    return jnp.stack(results)[None]


def solution(mesh):
    in_specs = (
        P("pipe", "ctx", None),
        P("ctx", None),
        P("pipe", None, None),
        P("pipe", None, None),
        P("pipe", None, "ctx", None),
        P(None, "ctx"),
        P(),
    )
    out_specs = P("pipe", None, "ctx", None)
    return jax.shard_map(body, mesh=mesh, in_specs=in_specs, out_specs=out_specs, check_vma=False)
```

profile of v0, /device:TPU:6, one launch (start us, length us, event | category | flops | bytes accessed | tf_op | source)
XLA Modules:
  0.0 61.1 jit_solution(8439224875971504812)
XLA Ops:
  0.0 1.2 %convert_reduce_fusion.1 = f32[128]{0:T(128)S(1)} fusion(bf16[1,128,1024]{2,1,0:T(8,128)(2,1)} %param.7), kind=kLoop, calls=%fused_computation.27 | loop fusion | flops 262016 | bytes 262656 | tf_op jit(solution)/shard_map/reduce_sum | solution.py:19
  1.2 1.2 %fusion.21 = f32[128]{0:T(128)S(1)} fusion(bf16[1,128,1024]{2,1,0:T(8,128)(2,1)} %param.7, f32[128]{0:T(128)S(1)} %broadcast_multiply_fusion.3), kind=kLoop, calls=%fused_computation.34 | loop fusion | flops 524160 | bytes 263168 | tf_op jit(solution)/shard_map/reduce_sum | solution.py:21
  2.3 0.8 %fusion.78 = (s32[128]{0:T(128)S(1)}, s32[128]{0:T(128)S(1)}) fusion(s32[5,128]{1,0:T(8,128)} %param.12, s32[]{:T(128)S(6)} %select_n.21, s32[]{:T(128)S(6)} %select_n.18), kind=kLoop, calls=%fused_computation.102 | loop fusion | bytes 2056 | tf_op jit(solution)/shard_map/eq | solution.py:84
  3.1 1.0 %dynamic-slice_reduce_fusion = (s32[4]{0:T(128)S(1)}, s32[4]{0:T(128)S(1)}) fusion(s32[5,4]{0,1:T(4,128)} %param.13, s32[]{:T(128)S(6)} %select_n.21, s32[]{:T(128)S(6)} %select_n.18), kind=kLoop, calls=%fused_computation.94 | loop fusion | bytes 72 | tf_op jit(solution)/shard_map/jit(dynamic_index_in_dim)/dynamic_slice | solution.py:77
  4.1 0.2 reduce-window.9
  4.6 0.9 %copy.51 = bf16[1,2,16,1024]{3,1,0,2:T(2,128)(2,1)S(1)} copy(bf16[1,2,16,1024]{3,2,1,0:T(8,128)(2,1)} %param.11) | data formatting | bytes 131072 | tf_op args[4]
  5.6 31.8 %all-gather = bf16[1,2,128,1024]{3,1,0,2:T(2,128)(2,1)S(1)} all-gather(bf16[1,2,16,1024]{3,1,0,2:T(2,128)(2,1)S(1)} %copy.51), channel_id=2, replica_groups=mesh['pipe'=4,'ctx'=8] {'ctx'}, dimensions={2}, use_global_device_ids=true | all-gather | bytes 589824 | tf_op jit(solution)/shard_map/all_gather | solution.py:66
  37.3 3.1 %multiply_convert_fusion.1 = bf16[128,2048]{1,0:T(8,128)(2,1)S(1)} fusion(bf16[1,1024,2048]{2,1,0:T(8,128)(2,1)} %param.9, bf16[1,128,1024]{2,1,0:T(8,128)(2,1)} %param.7, f32[128]{0:T(128)S(1)} %add_rsqrt_fusion.3, f32[128]{0:T(128)S(1)} %broadcast_multiply_fusion.3), kind=kOutput, calls=%fused_computation.22 | convolution fusion | flops 538705920 | bytes 4981760 | tf_op jit(solution)/shard_map/dot_general | solution.py:80
  40.4 0.7 %slice_bitcast_fusion.3 = (bf16[16,4,8,128]{3,2,1,0:T(8,128)(2,1)}, bf16[16,4,8,128]{3,2,1,0:T(8,128)(2,1)}, bf16[128,512]{1,0:T(8,128)(2,1)S(1)}) fusion(bf16[128,2048]{1,0:T(8,128)(2,1)S(1)} %multiply_convert_fusion.1), kind=kLoop, calls=%fused_computation.65 | loop fusion | bytes 786432
  41.3 0.7 %fusion.87 = (bf16[1,1,128,1024]{3,1,0,2:T(2,128)(2,1)S(1)}, bf16[1,1,128,1024]{3,1,0,2:T(2,128)(2,1)S(1)}) fusion(bf16[1,2,128,1024]{3,1,0,2:T(2,128)(2,1)S(1)} %all-gather), kind=kLoop, calls=%fused_computation.121 | loop fusion | bytes 1048576 | tf_op jit(solution)/shard_map/slice | solution.py:86
  42.0 0.4 copy.69
  42.5 0.7 %compare_convert_fusion = (f32[128,128]{1,0:T(8,128)}, f32[128,128]{1,0:T(8,128)}, f32[128,128]{1,0:T(8,128)S(1)}, f32[128,128]{1,0:T(8,128)S(1)}) fusion(s32[128]{0:T(128)S(1)} %convert_reduce_fusion.2, s32[128]{0:T(128)S(1)} %get-tuple-element.57, s32[128]{0:T(128)S(1)} %get-tuple-element.58, s32[128]{0:T(128)S(1)} %convert_reduce_fusion.3), kind=kLoop, calls=%fused_computation.91 | loop fusion | flops 180224 | bytes 264192 | tf_op jit(solution)/shard_map/while/body/eval_jaxpr/convert_element_type | solution.py:37
  43.3 2.1 %convolution_bitcast_fusion.3 = f32[128,4,128]{0,2,1:T(8,128)} fusion(bf16[128,4,128]{0,2,1:T(8,128)(2,1)S(1)} %bitcast.109, bf16[16,4,8,128]{3,2,1,0:T(8,128)(2,1)} %get-tuple-element.50, f32[128,128]{1,0:T(8,128)S(1)} %get-tuple-element.67, bf16[16,4,8,128]{3,2,1,0:T(8,128)(2,1)} %get-tuple-element.48), kind=kOutput, calls=%fused_computation.17 | convolution fusion | flops 34013184 | bytes 720896 | tf_op jit(solution)/shard_map/htn,nhd->thd/dot_general | solution.py:38
  45.3 1.4 %fusion.90 = (f32[128]{0:T(128)S(1)}, f32[128,4,128]{0,2,1:T(8,128)S(1)}) fusion(f32[128,4,128]{0,2,1:T(8,128)} %convolution_bitcast_fusion.3, bf16[128,4,128]{0,2,1:T(8,128)(2,1)S(1)} %bitcast.114, bf16[128,4,128]{0,2,1:T(8,128)(2,1)S(1)} %bitcast.113, f32[128,128]{1,0:T(8,128)S(1)} %get-tuple-element.68, bf16[16,4,8,128]{3,2,1,0:T(8,128)(2,1)} %get-tuple-element.48), kind=kOutput, calls=%fused_computation.124 | convolution fusion | flops 34144128 | bytes 983552 | tf_op jit(solution)/shard_map/while/body/eval_jaxpr/htn,nhd->thd/dot_general | solution.py:38
  47.0 0.4 fusion.4
  47.4 1.9 %collective-permute-start = (bf16[128,1024]{1,0:T(8,128)(2,1)S(1)}, bf16[128,1024]{1,0:T(8,128)(2,1)S(1)}, u32[]{:S(2)}, u32[]{:S(2)}) collective-permute-start(bf16[128,1024]{1,0:T(8,128)(2,1)S(1)} %fusion.4), channel_id=1, source_target_pairs={{0,8},{8,16},{16,24},{1,9},{9,17},{17,25},{2,10},{10,18},{18,26},{... | collective-permute-start | bytes 786440 | tf_op jit(solution)/shard_map/ppermute | solution.py:15
  49.4 0.4 copy.70
  49.8 5.3 %collective-permute-done = bf16[128,1024]{1,0:T(8,128)(2,1)S(1)} collective-permute-done((bf16[128,1024]{1,0:T(8,128)(2,1)S(1)}, bf16[128,1024]{1,0:T(8,128)(2,1)S(1)}, u32[]{:S(2)}, u32[]{:S(2)}) %collective-permute-start) | collective-permute-done | bytes 262176 | tf_op jit(solution)/shard_map/ppermute | solution.py:15
  55.3 0.2 fusion.18
  55.5 3.1 %multiply_convert_fusion = bf16[128,2048]{1,0:T(8,128)(2,1)S(1)} fusion(bf16[1,1024,2048]{2,1,0:T(8,128)(2,1)} %param.9, bf16[128,1024]{1,0:T(8,128)(2,1)S(1)} %get-tuple-element.36, f32[128]{0:T(128)S(1)} %add_rsqrt_fusion.1, f32[128]{0:T(128)S(1)} %broadcast_multiply_fusion.2), kind=kOutput, calls=%fused_computation.21 | convolution fusion | flops 538705920 | bytes 4981760 | tf_op jit(solution)/shard_map/dot_general | solution.py:80
  58.8 0.4 convolution_bitcast_fusion.1
  59.2 0.4 fusion.93
  59.9 0.4 fusion.8
  60.2 0.8 %maximum_bitcast_fusion = bf16[1,2,128,1024]{3,2,1,0:T(8,128)(2,1)} fusion(bf16[1,128,1024]{2,1,0:T(8,128)(2,1)S(1)} %fusion.8, bf16[1,128,1024]{2,1,0:T(8,128)(2,1)S(1)} %bitcast.106), kind=kLoop, calls=%fused_computation.37 | loop fusion | flops 262144 | bytes 1048576 | tf_op jit(solution)/shard_map/broadcast_in_dim | solution.py:94
  (33 shorter events, 1.4 us)
Async XLA Ops:
  0.0 47.0 %copy-start = (bf16[1,512,1024]{2,1,0:T(8,128)(2,1)S(1)}, bf16[1,512,1024]{2,1,0:T(8,128)(2,1)}, u32[]{:S(2)}) copy-start(bf16[1,512,1024]{2,1,0:T(8,128)(2,1)} %param.10) | copy-start | bytes 3145732
  41.2 5.9 %copy-start.1 = (bf16[1,128,1024]{2,1,0:T(8,128)(2,1)S(1)}, bf16[1,128,1024]{2,1,0:T(8,128)(2,1)}, u32[]{:S(2)}) copy-start(bf16[1,128,1024]{2,1,0:T(8,128)(2,1)} %param.7) | copy-start | bytes 786436
  42.5 12.6 %copy-start.2 = (bf16[128,1024]{1,0:T(8,128)(2,1)S(1)}, bf16[128,1024]{1,0:T(8,128)(2,1)}, u32[]{:S(2)}) copy-start(bf16[128,1024]{1,0:T(8,128)(2,1)} %param.8) | copy-start | bytes 786436
  47.4 7.7 %collective-permute-start = (bf16[128,1024]{1,0:T(8,128)(2,1)S(1)}, bf16[128,1024]{1,0:T(8,128)(2,1)S(1)}, u32[]{:S(2)}, u32[]{:S(2)}) collective-permute-start(bf16[128,1024]{1,0:T(8,128)(2,1)S(1)} %fusion.4), channel_id=1, source_target_pairs={{0,8},{8,16},{16,24},{1,9},{9,17},{17,25},{2,10},{10,18},{18,26},{... | collective-permute-start | bytes 786440 | tf_op jit(solution)/shard_map/ppermute | solution.py:15
  55.5 3.3 %copy-start.4 = (f32[128,128]{1,0:T(8,128)S(1)}, f32[128,128]{1,0:T(8,128)}, u32[]{:S(2)}) copy-start(f32[128,128]{1,0:T(8,128)} %get-tuple-element.60) | copy-start | bytes 196612
  55.5 3.7 %copy-start.3 = (f32[128,128]{1,0:T(8,128)S(1)}, f32[128,128]{1,0:T(8,128)}, u32[]{:S(2)}) copy-start(f32[128,128]{1,0:T(8,128)} %get-tuple-element.59) | copy-start | bytes 196612
where the time goes:
time: 61.4 us; the launch traced here: 61.1 us
  blocking collectives  31.8 us (52%)
  matrix products  11.2 us (18%)
  local copies, waits for them, and re-layouts  5.62 us (9%)
  waiting for transfers between devices  5.28 us (9%)
  other arithmetic  5.05 us (8%)
  starting transfers between devices  1.92 us (3%)
    all_gather x1, blocking collectives, body(): fetched = lax.all_gather(cache_kv[0], 'ctx', axis=1, tiled=True)  31.8 us
    dot_general x2, matrix products, body(): jnp.dot(normed, weights_in, preferred_element_type=jnp.float32)  6.18 us
    ppermute x1, waiting for transfers between devices, passed_along(): return lax.ppermute(block, axis, route)  5.28 us
    dot_general x4, matrix products, attend(): jnp.einsum('htn,nhd->thd', weights, value_part, preferred_element_type=jn...  4.31 us
    unnamed x15, local copies, waits for them, and re-layouts  2.59 us
    ppermute x1, starting transfers between devices, passed_along(): return lax.ppermute(block, axis, route)  1.92 us
    reduce_sum x4, other arithmetic, normalize(): spread = jnp.mean(shifted * shifted, axis=-1, keepdims=True)  1.56 us
    reduce_sum x2, other arithmetic, normalize(): center = jnp.mean(values, axis=-1, keepdims=True)  1.31 us
  transfers between devices with their start and end apart: 1, of which 1 were waited for; matrix products, arithmetic and copies ran while one was open for 1% of the time, Pallas kernels for 0%

commit v1 on v0

v1 whole, which is shorter than its diff:
```python
import functools

import jax
import jax.numpy as jnp
from jax import lax
from jax.experimental import pallas as pl
from jax.experimental.pallas import tpu as pltpu
from jax.sharding import PartitionSpec as P

HEADS = 4
STEPS = 2
CHUNKS = 4
MESH = pl.DeviceIdType.MESH


def normalize(values):
    center = jnp.mean(values, axis=-1, keepdims=True)
    shifted = values - center
    spread = jnp.mean(shifted * shifted, axis=-1, keepdims=True)
    return shifted * lax.rsqrt(spread + 1e-06)


def silu(values):
    half = 0.5 * values
    return half + half * jnp.tanh(half)


def kernel(
    sections, n, stride,
    incoming, fresh, w_in, w_out, cache, users_ref, lengths_ref,
    out,
    x_buf, w_buf, wo_buf, kv, q_buf, result,
    load_sem, w_sem, out_sem, own_sem, cache_send, cache_recv, relay_send, relay_recv,
):
    section = lax.axis_index("pipe")
    me = lax.axis_index("ctx")
    rows = x_buf.shape[1]
    width = wo_buf.shape[0]
    depth = wo_buf.shape[1]
    piece = depth // CHUNKS
    part = cache.shape[2]
    cached = n * part
    head = width // HEADS
    lines = n // stride
    first = section == 0
    last = section == sections - 1

    x_load = pltpu.make_async_copy(incoming.at[0], x_buf.at[0], load_sem.at[0])
    x_load.start()
    fresh_load = pltpu.make_async_copy(fresh, x_buf.at[1], load_sem.at[1])

    @pl.when(first)
    def _():
        fresh_load.start()

    def w_load(block):
        columns = pl.ds(block * width, width)
        return pltpu.make_async_copy(
            w_in.at[0, :, columns], w_buf.at[:, columns], w_sem.at[block]
        )

    wo_load = pltpu.make_async_copy(w_out.at[0], wo_buf, load_sem.at[2])
    for block in (2, 3, 1, 0):
        w_load(block).start()
    wo_load.start()

    def place(owner):
        return pl.ds(pl.multiple_of(owner * part, part), part)

    own = [
        pltpu.make_async_copy(cache.at[0, t], kv.at[t, place(me), :], own_sem.at[t])
        for t in range(STEPS)
    ]
    for copy in own:
        copy.start()

    lane = lax.rem(me, stride)
    group = me - lane

    def along(hop):
        return lax.rem(me + hop * stride, n)

    def beside(hop):
        return group + lax.rem(lane + hop, stride)

    barrier = pltpu.get_barrier_semaphore()
    for hop in range(1, lines):
        pl.semaphore_signal(barrier, inc=1, device_id={"ctx": along(hop)}, device_id_type=MESH)
    for hop in range(1, stride):
        pl.semaphore_signal(barrier, inc=1, device_id={"ctx": beside(hop)}, device_id_type=MESH)

    @pl.when(jnp.logical_not(last))
    def _():
        pl.semaphore_signal(barrier, inc=1, device_id={"pipe": section + 1}, device_id_type=MESH)

    @pl.when(jnp.logical_not(first))
    def _():
        pl.semaphore_signal(barrier, inc=1, device_id={"pipe": section - 1}, device_id_type=MESH)

    ends = jnp.where(first, 1, 0) + jnp.where(last, 1, 0)
    pl.semaphore_wait(barrier, lines - 1 + stride - 1 + 2 - ends)

    def spread(t, hop):
        slot = hop * stride
        return pltpu.make_async_remote_copy(
            src_ref=cache.at[0, t],
            dst_ref=kv.at[t, place(me), :],
            send_sem=cache_send.at[t, slot],
            recv_sem=cache_recv.at[t, slot],
            device_id={"ctx": along(hop)},
            device_id_type=MESH,
        )

    def spread_arrival(t, hop):
        slot = hop * stride
        owner = lax.rem(me + (lines - hop) * stride, n)
        return pltpu.make_async_remote_copy(
            src_ref=cache.at[0, t],
            dst_ref=kv.at[t, place(owner), :],
            send_sem=cache_send.at[t, slot],
            recv_sem=cache_recv.at[t, slot],
            device_id={"ctx": along(hop)},
            device_id_type=MESH,
        )

    def forward(t, hop, side):
        slot = hop * stride + side
        owner = lax.rem(me + (lines - hop) * stride, n)
        source = cache.at[0, t] if hop == 0 else kv.at[t, place(owner), :]
        return pltpu.make_async_remote_copy(
            src_ref=source,
            dst_ref=kv.at[t, place(owner), :],
            send_sem=cache_send.at[t, slot],
            recv_sem=cache_recv.at[t, slot],
            device_id={"ctx": beside(side)},
            device_id_type=MESH,
        )

    def forward_arrival(t, hop, side):
        slot = hop * stride + side
        owner = lax.rem(beside(stride - side) + (lines - hop) * stride, n)
        return pltpu.make_async_remote_copy(
            src_ref=cache.at[0, t],
            dst_ref=kv.at[t, place(owner), :],
            send_sem=cache_send.at[t, slot],
            recv_sem=cache_recv.at[t, slot],
            device_id={"ctx": beside(side)},
            device_id_type=MESH,
        )

    def send_own(t):
        for hop in range(1, lines):
            spread(t, hop).start()
        for side in range(1, stride):
            forward(t, 0, side).start()

    def pass_on(t):
        for hop in range(1, lines):
            spread_arrival(t, hop).wait_recv()
            for side in range(1, stride):
                forward(t, hop, side).start()

    def arrived(t):
        own[t].wait()
        for hop in range(lines):
            for side in range(1, stride):
                forward_arrival(t, hop, side).wait_recv()

    def relay(c):
        columns = pl.ds(c * piece, piece)
        return pltpu.make_async_remote_copy(
            src_ref=result.at[0, :, columns],
            dst_ref=x_buf.at[1, :, columns],
            send_sem=relay_send.at[c],
            recv_sem=relay_recv.at[c],
            device_id={"pipe": lax.rem(section + 1, sections)},
            device_id_type=MESH,
        )

    def store(t):
        return pltpu.make_async_copy(result.at[t], out.at[0, t], out_sem.at[t])

    def project(normed, block):
        return silu(
            jnp.dot(
                normed,
                w_buf[:, block * width : (block + 1) * width],
                preferred_element_type=jnp.float32,
            )
        ).astype(jnp.bfloat16)

    def allowed_rows(t):
        batch = sections - 1 - section + t
        users = jnp.broadcast_to(users_ref[pl.ds(batch, 1), :], (rows, rows))
        mine = users.T
        row = lax.broadcasted_iota(jnp.int32, (rows, rows), 0)
        column = lax.broadcasted_iota(jnp.int32, (rows, rows), 1)
        new = jnp.where((users == mine) & (column <= row), 1.0, 0.0)
        position = lax.broadcasted_iota(jnp.int32, (rows, cached), 1)
        owner = jnp.zeros((rows, cached), jnp.int32)
        bound = jnp.int32(0)
        for user in range(lengths_ref.shape[1] - 1):
            bound = bound + lengths_ref[batch, user]
            owner = owner + jnp.where(position >= bound, 1, 0)
        old = jnp.where(owner == mine[:, :1], 1.0, 0.0)
        return jnp.concatenate([old, new], axis=1)

    send_own(0)
    for t in range(STEPS):
        allowed = allowed_rows(t)
        if t == 0:
            x_load.wait()
        else:
            @pl.when(first)
            def _():
                fresh_load.wait()

            @pl.when(jnp.logical_not(first))
            def _():
                for c in range(CHUNKS):
                    relay(c).wait_recv()

        normed = normalize(x_buf[t].astype(jnp.float32)).astype(jnp.bfloat16)
        for block, into in ((2, 0), (3, 1)):
            if t == 0:
                w_load(block).wait()
            kv[t, cached:, into * width : (into + 1) * width] = project(normed, block)
        if t == 0:
            pass_on(0)
            send_own(1)
            w_load(1).wait()
        q_buf[...] = project(normed, 1)
        if t == 0:
            w_load(0).wait()
        gate = project(normed, 0)
        arrived(t)
        heads = []
        for h in range(HEADS):
            low, high = h * head, (h + 1) * head
            scores = lax.dot_general(
                q_buf[:, low:high],
                kv[t, :, low:high],
                (((1,), (1,)), ((), ())),
                preferred_element_type=jnp.float32,
            )
            weights = (silu(head ** (-0.5) * scores) * allowed).astype(jnp.bfloat16)
            heads.append(
                jnp.dot(
                    weights,
                    kv[t, :, width + low : width + high],
                    preferred_element_type=jnp.float32,
                )
            )
        attn = jnp.concatenate(heads, axis=1)
        mixed = (normalize(attn) * gate.astype(jnp.float32)).astype(jnp.bfloat16)
        if t == 0:
            wo_load.wait()
        for c in range(CHUNKS):
            low, high = c * piece, (c + 1) * piece
            result[t, :, low:high] = (
                jnp.dot(mixed, wo_buf[:, low:high], preferred_element_type=jnp.float32)
                + x_buf[t, :, low:high].astype(jnp.float32)
            ).astype(jnp.bfloat16)
            if t == 0:
                @pl.when(jnp.logical_not(last))
                def _():
                    relay(c).start()
        store(t).start()
        if t == 0:
            pass_on(1)

    for t in range(STEPS):
        store(t).wait()
        for hop in range(lines):
            if hop > 0:
                spread(t, hop).wait_send()
            for side in range(1, stride):
                forward(t, hop, side).wait_send()

    @pl.when(jnp.logical_not(last))
    def _():
        for c in range(CHUNKS):
            relay(c).wait_send()


def body(incoming, fresh, w_uvqk, w_out, cache_kv, rows_user, cache_len):
    sections = lax.axis_size("pipe")
    n = lax.axis_size("ctx")
    stride = 2 if n % 2 == 0 else 1
    rows, depth = fresh.shape
    width = w_out.shape[1]
    part = cache_kv.shape[2]
    anywhere = pl.BlockSpec(memory_space=pl.ANY)
    dma = pltpu.SemaphoreType.DMA
    return pl.pallas_call(
        functools.partial(kernel, sections, n, stride),
        out_shape=jax.ShapeDtypeStruct((1, STEPS, rows, depth), jnp.bfloat16),
        in_specs=[anywhere] * 5
        + [
            pl.BlockSpec(memory_space=pltpu.VMEM),
            pl.BlockSpec(memory_space=pltpu.SMEM),
        ],
        out_specs=anywhere,
        scratch_shapes=[
            pltpu.VMEM((STEPS, rows, depth), jnp.bfloat16),
            pltpu.VMEM((depth, 4 * width), jnp.bfloat16),
            pltpu.VMEM((width, depth), jnp.bfloat16),
            pltpu.VMEM((STEPS, n * part + rows, 2 * width), jnp.bfloat16),
            pltpu.VMEM((rows, width), jnp.bfloat16),
            pltpu.VMEM((STEPS, rows, depth), jnp.bfloat16),
            dma((3,)),
            dma((4,)),
            dma((STEPS,)),
            dma((STEPS,)),
            dma((STEPS, n)),
            dma((STEPS, n)),
            dma((CHUNKS,)),
            dma((CHUNKS,)),
        ],
        compiler_params=pltpu.CompilerParams(
            collective_id=0, has_side_effects=True, vmem_limit_bytes=40 * 2**20
        ),
    )(incoming, fresh, w_uvqk, w_out, cache_kv, rows_user, cache_len)


def solution(mesh):
    in_specs = (
        P("pipe", "ctx", None),
        P("ctx", None),
        P("pipe", None, None),
        P("pipe", None, None),
        P("pipe", None, "ctx", None),
        P(None, "ctx"),
        P(),
    )
    out_specs = P("pipe", None, "ctx", None)
    return jax.shard_map(body, mesh=mesh, in_specs=in_specs, out_specs=out_specs, check_vma=False)
```

time: 61.4 us -> 29.5 us (0.48)
  the two profiles are of different devices: /device:TPU:6 before, /device:TPU:0 now
where the time goes in v1:
time: 29.5 us; the launch traced here: 29.2 us
  Pallas kernels  20.8 us (71%)
  local copies, waits for them, and re-layouts  8.4 us (28%)
    pallas_call x1, Pallas kernels, body(): pl.pallas_call(functools.partial(kernel, sections, n, stride), out_shape=...  20.8 us
    unnamed x14, local copies, waits for them, and re-layouts  8.4 us

profile of v1, /device:TPU:0, one launch (start us, length us, event | category | flops | bytes accessed | tf_op | source)
XLA Modules:
  0.0 29.2 jit_solution(8966856748031528020)
XLA Ops:
  0.0 0.8 %copy.8.lengths_ref = s32[5,4]{1,0:T(8,128)S(1)} copy(s32[5,4]{0,1:T(4,128)} %param.13) | data formatting | bytes 160 | tf_op args[6]
  0.8 0.0 copy-start
  0.8 2.2 %copy-done = bf16[1,1024,2048]{2,1,0:T(8,128)(2,1)S(1)} copy-done((bf16[1,1024,2048]{2,1,0:T(8,128)(2,1)S(1)}, bf16[1,1024,2048]{2,1,0:T(8,128)(2,1)}, u32[]{:S(2)}) %copy-start) | copy-done | bytes 4194328
  3.0 0.0 copy-start.1
  3.0 1.2 %copy-done.1 = bf16[1,512,1024]{2,1,0:T(8,128)(2,1)S(1)} copy-done((bf16[1,512,1024]{2,1,0:T(8,128)(2,1)S(1)}, bf16[1,512,1024]{2,1,0:T(8,128)(2,1)}, u32[]{:S(2)}) %copy-start.1) | copy-done | bytes 1048600
  4.2 0.0 copy-start.2
  4.2 0.9 %copy-done.2 = bf16[1,128,1024]{2,1,0:T(8,128)(2,1)S(1)} copy-done((bf16[1,128,1024]{2,1,0:T(8,128)(2,1)S(1)}, bf16[1,128,1024]{2,1,0:T(8,128)(2,1)}, u32[]{:S(2)}) %copy-start.2) | copy-done | bytes 262168
  5.1 0.0 copy-start.3
  5.1 0.9 %copy-done.3 = bf16[128,1024]{1,0:T(8,128)(2,1)S(1)} copy-done((bf16[128,1024]{1,0:T(8,128)(2,1)S(1)}, bf16[128,1024]{1,0:T(8,128)(2,1)}, u32[]{:S(2)}) %copy-start.3) | copy-done | bytes 262168
  6.1 0.0 copy-start.4
  6.1 0.8 %copy-done.4 = bf16[1,2,16,1024]{3,2,1,0:T(8,128)(2,1)S(1)} copy-done((bf16[1,2,16,1024]{3,2,1,0:T(8,128)(2,1)S(1)}, bf16[1,2,16,1024]{3,2,1,0:T(8,128)(2,1)}, u32[]{:S(2)}) %copy-start.4) | copy-done | bytes 65560
  6.9 0.0 copy-start.5
  6.9 0.7 %copy-done.5 = s32[5,128]{1,0:T(8,128)S(1)} copy-done((s32[5,128]{1,0:T(8,128)S(1)}, s32[5,128]{1,0:T(8,128)}, u32[]{:S(2)}) %copy-start.5) | copy-done | bytes 2584
  7.6 20.8 %shard_map.73 = bf16[1,2,128,1024]{3,2,1,0:T(8,128)(2,1)S(1)} custom-call(bf16[1,128,1024]{2,1,0:T(8,128)(2,1)S(1)} %copy-done.2, bf16[128,1024]{1,0:T(8,128)(2,1)S(1)} %copy-done.3, bf16[1,1024,2048]{2,1,0:T(8,128)(2,1)S(1)} %copy-done, bf16[1,512,1024]{2,1,0:T(8,128)(2,1)S(1)} %copy-done.1, bf16[1,2,16,1024]{3,2,1,0:T(8,128)(2,1)S(1)} %copy-done.4, ...), custom_call_target="tpu_custom_call" | custom-call | tf_op jit(solution)/shard_map/pallas_call | solution.py:295
  28.4 0.8 %copy.10 = bf16[1,2,128,1024]{3,2,1,0:T(8,128)(2,1)} copy(bf16[1,2,128,1024]{3,2,1,0:T(8,128)(2,1)S(1)} %shard_map.73) | data formatting | bytes 1048576
Async XLA Ops:
  0.8 2.2 %copy-start = (bf16[1,1024,2048]{2,1,0:T(8,128)(2,1)S(1)}, bf16[1,1024,2048]{2,1,0:T(8,128)(2,1)}, u32[]{:S(2)}) copy-start(bf16[1,1024,2048]{2,1,0:T(8,128)(2,1)} %w_in.1) | copy-start | bytes 12582916
  3.0 1.2 %copy-start.1 = (bf16[1,512,1024]{2,1,0:T(8,128)(2,1)S(1)}, bf16[1,512,1024]{2,1,0:T(8,128)(2,1)}, u32[]{:S(2)}) copy-start(bf16[1,512,1024]{2,1,0:T(8,128)(2,1)} %w_out.1) | copy-start | bytes 3145732
  4.2 0.9 %copy-start.2 = (bf16[1,128,1024]{2,1,0:T(8,128)(2,1)S(1)}, bf16[1,128,1024]{2,1,0:T(8,128)(2,1)}, u32[]{:S(2)}) copy-start(bf16[1,128,1024]{2,1,0:T(8,128)(2,1)} %incoming.1) | copy-start | bytes 786436
  5.1 0.9 %copy-start.3 = (bf16[128,1024]{1,0:T(8,128)(2,1)S(1)}, bf16[128,1024]{1,0:T(8,128)(2,1)}, u32[]{:S(2)}) copy-start(bf16[128,1024]{1,0:T(8,128)(2,1)} %fresh.1) | copy-start | bytes 786436
  6.1 0.8 %copy-start.4 = (bf16[1,2,16,1024]{3,2,1,0:T(8,128)(2,1)S(1)}, bf16[1,2,16,1024]{3,2,1,0:T(8,128)(2,1)}, u32[]{:S(2)}) copy-start(bf16[1,2,16,1024]{3,2,1,0:T(8,128)(2,1)} %cache.1) | copy-start | bytes 196612
  6.9 0.7 %copy-start.5 = (s32[5,128]{1,0:T(8,128)S(1)}, s32[5,128]{1,0:T(8,128)}, u32[]{:S(2)}) copy-start(s32[5,128]{1,0:T(8,128)} %users_ref.1) | copy-start | bytes 7684

commit v2 on v1

--- a/solution.py
+++ b/solution.py
@@ -27,10 +27,10 @@
 
 def kernel(
     sections, n, stride,
-    incoming, fresh, w_in, w_out, cache, users_ref, lengths_ref,
-    out,
-    x_buf, w_buf, wo_buf, kv, q_buf, result,
-    load_sem, w_sem, out_sem, own_sem, cache_send, cache_recv, relay_send, relay_recv,
+    incoming, fresh, w_in, w_out, cache, users_in, lengths_in,
+    result,
+    x_buf, w_buf, wo_buf, kv, q_buf, users_ref, lengths_ref,
+    load_sem, w_sem, own_sem, cache_send, cache_recv, relay_send, relay_recv,
 ):
     section = lax.axis_index("pipe")
     me = lax.axis_index("ctx")
@@ -47,6 +47,10 @@
 
     x_load = pltpu.make_async_copy(incoming.at[0], x_buf.at[0], load_sem.at[0])
     x_load.start()
+    users_load = pltpu.make_async_copy(users_in, users_ref, load_sem.at[3])
+    lengths_load = pltpu.make_async_copy(lengths_in, lengths_ref, load_sem.at[4])
+    users_load.start()
+    lengths_load.start()
     fresh_load = pltpu.make_async_copy(fresh, x_buf.at[1], load_sem.at[1])
 
     @pl.when(first)
@@ -169,16 +173,13 @@
     def relay(c):
         columns = pl.ds(c * piece, piece)
         return pltpu.make_async_remote_copy(
-            src_ref=result.at[0, :, columns],
+            src_ref=result.at[0, 0, :, columns],
             dst_ref=x_buf.at[1, :, columns],
             send_sem=relay_send.at[c],
             recv_sem=relay_recv.at[c],
             device_id={"pipe": lax.rem(section + 1, sections)},
             device_id_type=MESH,
         )
-
-    def store(t):
-        return pltpu.make_async_copy(result.at[t], out.at[0, t], out_sem.at[t])
 
     def project(normed, block):
         return silu(
@@ -199,13 +200,16 @@
         position = lax.broadcasted_iota(jnp.int32, (rows, cached), 1)
         owner = jnp.zeros((rows, cached), jnp.int32)
         bound = jnp.int32(0)
-        for user in range(lengths_ref.shape[1] - 1):
-            bound = bound + lengths_ref[batch, user]
+        for user in range(lengths_ref.shape[0] - 1):
+            bound = bound + lengths_ref[user, batch]
             owner = owner + jnp.where(position >= bound, 1, 0)
         old = jnp.where(owner == mine[:, :1], 1.0, 0.0)
         return jnp.concatenate([old, new], axis=1)
 
     send_own(0)
+    send_own(1)
+    users_load.wait()
+    lengths_load.wait()
     for t in range(STEPS):
         allowed = allowed_rows(t)
         if t == 0:
@@ -227,7 +231,6 @@
             kv[t, cached:, into * width : (into + 1) * width] = project(normed, block)
         if t == 0:
             pass_on(0)
-            send_own(1)
             w_load(1).wait()
         q_buf[...] = project(normed, 1)
         if t == 0:
@@ -257,7 +260,7 @@
             wo_load.wait()
         for c in range(CHUNKS):
             low, high = c * piece, (c + 1) * piece
-            result[t, :, low:high] = (
+            result[0, t, :, low:high] = (
                 jnp.dot(mixed, wo_buf[:, low:high], preferred_element_type=jnp.float32)
                 + x_buf[t, :, low:high].astype(jnp.float32)
             ).astype(jnp.bfloat16)
@@ -265,12 +268,10 @@
                 @pl.when(jnp.logical_not(last))
                 def _():
                     relay(c).start()
-        store(t).start()
         if t == 0:
             pass_on(1)
 
     for t in range(STEPS):
-        store(t).wait()
         for hop in range(lines):
             if hop > 0:
                 spread(t, hop).wait_send()
@@ -290,27 +291,23 @@
     rows, depth = fresh.shape
     width = w_out.shape[1]
     part = cache_kv.shape[2]
-    anywhere = pl.BlockSpec(memory_space=pl.ANY)
+    anywhere = pl.BlockSpec(memory_space=pltpu.HBM)
     dma = pltpu.SemaphoreType.DMA
     return pl.pallas_call(
         functools.partial(kernel, sections, n, stride),
         out_shape=jax.ShapeDtypeStruct((1, STEPS, rows, depth), jnp.bfloat16),
-        in_specs=[anywhere] * 5
-        + [
-            pl.BlockSpec(memory_space=pltpu.VMEM),
-            pl.BlockSpec(memory_space=pltpu.SMEM),
-        ],
-        out_specs=anywhere,
+        in_specs=[anywhere] * 7,
+        out_specs=pl.BlockSpec(memory_space=pltpu.VMEM),
         scratch_shapes=[
             pltpu.VMEM((STEPS, rows, depth), jnp.bfloat16),
             pltpu.VMEM((depth, 4 * width), jnp.bfloat16),
             pltpu.VMEM((width, depth), jnp.bfloat16),
             pltpu.VMEM((STEPS, n * part + rows, 2 * width), jnp.bfloat16),
             pltpu.VMEM((rows, width), jnp.bfloat16),
-            pltpu.VMEM((STEPS, rows, depth), jnp.bfloat16),
-            dma((3,)),
+            pltpu.VMEM(rows_user.shape, jnp.int32),
+            pltpu.SMEM(cache_len.shape[::-1], jnp.int32),
+            dma((5,)),
             dma((4,)),
-            dma((STEPS,)),
             dma((STEPS,)),
             dma((STEPS, n)),
             dma((STEPS, n)),
@@ -318,9 +315,9 @@
             dma((CHUNKS,)),
         ],
         compiler_params=pltpu.CompilerParams(
-            collective_id=0, has_side_effects=True, vmem_limit_bytes=40 * 2**20
+            collective_id=0, has_side_effects=True, vmem_limit_bytes=62 * 2**20
         ),
-    )(incoming, fresh, w_uvqk, w_out, cache_kv, rows_user, cache_len)
+    )(incoming, fresh, w_uvqk, w_out, cache_kv, rows_user, cache_len.T)
 
 
 def solution(mesh):

time: 29.5 us -> 21.8 us (0.74)
  local copies, waits for them, and re-layouts: 8.4 us -> 1.87 us
  Pallas kernels: 20.8 us -> 19.8 us
    unnamed x14 -> x1, local copies, waits for them, and re-layouts: 8.4 us -> 1.87 us
    pallas_call x1, Pallas kernels: 20.8 us -> 19.8 us  [body(): pl.pallas_call(functools.partial(kernel, sections, n, stride), out_shape=...]
where the time goes in v2:
time: 21.8 us; the launch traced here: 21.6 us
  Pallas kernels  19.8 us (91%)
  local copies, waits for them, and re-layouts  1.87 us (9%)
    pallas_call x1, Pallas kernels, body(): pl.pallas_call(functools.partial(kernel, sections, n, stride), out_shape=...  19.8 us
    unnamed x1, local copies, waits for them, and re-layouts  1.87 us

profile of v2, /device:TPU:0, one launch (start us, length us, event | category | flops | bytes accessed | tf_op | source)
XLA Modules:
  0.0 21.6 jit_solution(9169314545149748721)
XLA Ops:
  0.0 19.8 %shard_map.73 = bf16[1,2,128,1024]{3,2,1,0:T(8,128)(2,1)} custom-call(bf16[1,128,1024]{2,1,0:T(8,128)(2,1)} %incoming.1, bf16[128,1024]{1,0:T(8,128)(2,1)} %fresh.1, bf16[1,1024,2048]{2,1,0:T(8,128)(2,1)} %w_in.1, bf16[1,512,1024]{2,1,0:T(8,128)(2,1)} %w_out.1, bf16[1,2,16,1024]{3,2,1,0:T(8,128)(2,1)} %cache.1, s32[5,128]{1,0:T(8,128)} %users_in.1, ...), custom_call_target="tpu_custom_call" | custom-call | tf_op jit(solution)/shard_map/pallas_call | solution.py:296
  19.8 1.9 %copy.9 = bf16[1,2,128,1024]{3,2,1,0:T(8,128)(2,1)} copy(bf16[1,2,128,1024]{3,2,1,0:T(8,128)(2,1)} %shard_map.73) | data formatting | bytes 1048576

commit v3 on v2

--- a/solution.py
+++ b/solution.py
@@ -315,9 +315,14 @@
             dma((CHUNKS,)),
         ],
         compiler_params=pltpu.CompilerParams(
-            collective_id=0, has_side_effects=True, vmem_limit_bytes=62 * 2**20
+            collective_id=0, has_side_effects=True, vmem_limit_bytes=40 * 2**20
         ),
-    )(incoming, fresh, w_uvqk, w_out, cache_kv, rows_user, cache_len.T)
+    )(
+        *(
+            pltpu.with_memory_space_constraint(operand, pltpu.HBM)
+            for operand in (incoming, fresh, w_uvqk, w_out, cache_kv, rows_user, cache_len.T)
+        )
+    )
 
 
 def solution(mesh):

time: 21.8 us -> 19.9 us (0.913)
  local copies, waits for them, and re-layouts: 1.87 us -> 0.8 us
  Pallas kernels: 19.8 us -> 19 us
    unnamed x1, local copies, waits for them, and re-layouts: 1.87 us -> 0.8 us
    pallas_call x1, Pallas kernels: 19.8 us -> 19 us  [body(): pl.pallas_call(functools.partial(kernel, sections, n, stride), out_shape=...]
where the time goes in v3:
time: 19.9 us; the launch traced here: 19.8 us
  Pallas kernels  19 us (95%)
  local copies, waits for them, and re-layouts  0.8 us (4%)
    pallas_call x1, Pallas kernels, body(): pl.pallas_call(functools.partial(kernel, sections, n, stride), out_shape=...  19 us
    unnamed x1, local copies, waits for them, and re-layouts  0.8 us

profile of v3, /device:TPU:0, one launch (start us, length us, event | category | flops | bytes accessed | tf_op | source)
XLA Modules:
  0.0 19.8 jit_solution(1333337183206831165)
XLA Ops:
  0.0 19.0 %shard_map.73 = bf16[1,2,128,1024]{3,2,1,0:T(8,128)(2,1)S(1)} custom-call(bf16[1,128,1024]{2,1,0:T(8,128)(2,1)} %incoming.1, bf16[128,1024]{1,0:T(8,128)(2,1)} %fresh.1, bf16[1,1024,2048]{2,1,0:T(8,128)(2,1)} %w_in.1, bf16[1,512,1024]{2,1,0:T(8,128)(2,1)} %w_out.1, bf16[1,2,16,1024]{3,2,1,0:T(8,128)(2,1)} %cache.1, s32[5,128]{1,0:T(8,128)} %users_in.1, ...), custom_call_target="tpu_custom_call" | custom-call | tf_op jit(solution)/shard_map/pallas_call | solution.py:296
  19.0 0.8 %copy.9 = bf16[1,2,128,1024]{3,2,1,0:T(8,128)(2,1)} copy(bf16[1,2,128,1024]{3,2,1,0:T(8,128)(2,1)S(1)} %shard_map.73) | data formatting | bytes 1048576

commit v4 on v3

--- a/solution.py
+++ b/solution.py
@@ -64,9 +64,7 @@
         )
 
     wo_load = pltpu.make_async_copy(w_out.at[0], wo_buf, load_sem.at[2])
-    for block in (2, 3, 1, 0):
-        w_load(block).start()
-    wo_load.start()
+    w_load(2).start()
 
     def place(owner):
         return pl.ds(pl.multiple_of(owner * part, part), part)
@@ -207,6 +205,9 @@
         return jnp.concatenate([old, new], axis=1)
 
     send_own(0)
+    for block in (3, 1, 0):
+        w_load(block).start()
+    wo_load.start()
     send_own(1)
     users_load.wait()
     lengths_load.wait()

time: 19.9 us -> 19.9 us (level)
  no operation moved by 1% of the time
where the time goes in v4:
time: 19.9 us; the launch traced here: 19.8 us
  Pallas kernels  19 us (95%)
  local copies, waits for them, and re-layouts  0.8 us (4%)
    pallas_call x1, Pallas kernels, body(): pl.pallas_call(functools.partial(kernel, sections, n, stride), out_shape=...  19 us
    unnamed x1, local copies, waits for them, and re-layouts  0.8 us

profile of v4, /device:TPU:0, one launch (start us, length us, event | category | flops | bytes accessed | tf_op | source)
XLA Modules:
  0.0 19.8 jit_solution(12152929634389477545)
XLA Ops:
  0.0 19.0 %shard_map.73 = bf16[1,2,128,1024]{3,2,1,0:T(8,128)(2,1)S(1)} custom-call(bf16[1,128,1024]{2,1,0:T(8,128)(2,1)} %incoming.1, bf16[128,1024]{1,0:T(8,128)(2,1)} %fresh.1, bf16[1,1024,2048]{2,1,0:T(8,128)(2,1)} %w_in.1, bf16[1,512,1024]{2,1,0:T(8,128)(2,1)} %w_out.1, bf16[1,2,16,1024]{3,2,1,0:T(8,128)(2,1)} %cache.1, s32[5,128]{1,0:T(8,128)} %users_in.1, ...), custom_call_target="tpu_custom_call" | custom-call | tf_op jit(solution)/shard_map/pallas_call | solution.py:297
  19.0 0.8 %copy.9 = bf16[1,2,128,1024]{3,2,1,0:T(8,128)(2,1)} copy(bf16[1,2,128,1024]{3,2,1,0:T(8,128)(2,1)S(1)} %shard_map.73) | data formatting | bytes 1048576
